TPU v7x, 256 devices: a whole 4x4x8 slice. The times are simulated.
256 devices in a mesh: row: 16 (over y_lo, x, core), col: 8 (over z), occ: 2 (over y_hi).
Axes of the slice: x: 4, y: 4 (y_hi: 2, y_lo: 2; y = y_hi * 2 + y_lo), z: 8, core: 2. Of those that a mesh axis runs over, the one named last changes fastest.
Arguments:
- amplitudes: float32 [2, 16, 8, 15488], P(None, 'row', 'col'), may hold values from -6 to 6
- aux_factor: float32 [16, 16, 8, 15488], P('occ', 'row', 'col'), as said below
- virt_irrep: int32 [22], replicated, may hold values from 0 to 7
- pair_irrep: int32 [2], replicated, may hold values from 0 to 7
- aux_irrep: int32 [16], replicated, may hold values from 0 to 7
- block_pattern: int32 [22, 22], replicated, may hold values 0 or 1
Outputs:
- ladder: float32 [2, 16, 8, 15488], P('occ', 'row', 'col')
Inputs may be any that keep to these rules, and one draw needn't show every extreme that they name: aux_factor is symmetric in its two virtual indices: B[q, a, c] = B[q, c, a].
All inputs are finite; a program needn't handle non-finite values.
Results may differ from a plain program's by a relative error of at most 0.0001.
Values sent between devices are 32-bit elements; how exact they have to be, the bound alone decides.
A program may use at most 320 MiB of HBM per device.

v0:
```python
import jax
import jax.numpy as jnp
from jax import lax
from jax.sharding import PartitionSpec as P

VIRTUALS = 1408
BLOCK_WIDTH = 64


def block_onehot(indices, block_count):
    return indices[..., None] // BLOCK_WIDTH == jnp.arange(block_count, dtype=jnp.int32)


def label_lookup(hot_table, virt_irrep):
    return jnp.sum(jnp.where(hot_table, virt_irrep, 0), axis=-1)


def per_device(amplitudes, aux_factor, virt_irrep, pair_irrep, aux_irrep, block_pattern):
    tile_count = lax.axis_size("row")
    col_count = lax.axis_size("col")
    local_rows = VIRTUALS // tile_count
    sub_width = local_rows // col_count
    amplitudes = amplitudes.reshape(amplitudes.shape[0], local_rows, tile_count, sub_width)
    aux_factor = aux_factor.reshape(aux_factor.shape[0], local_rows, tile_count, sub_width)
    block_count = virt_irrep.shape[0]
    row_index = lax.axis_index("row") * local_rows + jnp.arange(local_rows, dtype=jnp.int32)
    col_index = (
        jnp.arange(tile_count, dtype=jnp.int32)[:, None] * local_rows
        + lax.axis_index("col") * sub_width
        + jnp.arange(sub_width, dtype=jnp.int32)[None, :]
    )
    row_hot = block_onehot(row_index, block_count)
    col_hot = block_onehot(col_index, block_count)
    product = jnp.bitwise_xor(
        label_lookup(row_hot, virt_irrep)[:, None, None], label_lookup(col_hot, virt_irrep)[None]
    )
    kept_mask = product[None] == pair_irrep[:, None, None, None]
    masked = jnp.where(kept_mask, amplitudes, 0.0)
    pattern = (block_pattern * block_pattern.T).astype(jnp.float32)
    screen = (
        jnp.einsum(
            "ak,kl,itl->ait", row_hot.astype(jnp.float32), pattern, col_hot.astype(jnp.float32)
        )
        > 0.5
    )
    aux_here = aux_factor.shape[0]
    aux_labels = lax.dynamic_slice_in_dim(aux_irrep, lax.axis_index("occ") * aux_here, aux_here, 0)
    aux_mask = jnp.logical_and(screen[None], product[None] == aux_labels[:, None, None, None])
    factor = jnp.where(aux_mask, aux_factor, 0.0)
    half_pairs = masked.shape[0] // lax.axis_size("occ")
    masked = lax.dynamic_slice_in_dim(masked, lax.axis_index("occ") * half_pairs, half_pairs, 0)
    factor = lax.all_gather(factor, "occ", axis=0, tiled=True)
    pair_count = masked.shape[0]
    aux_count = factor.shape[0]
    split_view = masked.reshape(pair_count, col_count, sub_width, tile_count, sub_width)
    swapped = lax.all_to_all(
        lax.all_to_all(split_view, "row", split_axis=3, concat_axis=3, tiled=True),
        "col",
        split_axis=1,
        concat_axis=4,
        tiled=True,
    )
    mirrored = swapped.reshape(pair_count, sub_width, tile_count, local_rows).transpose(0, 3, 2, 1)
    antisym = masked - mirrored
    columns = lax.all_gather(factor, "row", axis=1, tiled=True)
    columns = columns.reshape(aux_count, tile_count, local_rows, tile_count * sub_width)
    rows_panel = lax.all_gather(factor, "col", axis=3, tiled=True).reshape(
        aux_count, local_rows, tile_count * local_rows
    )
    chosen = columns
    contracted = jnp.einsum(
        "pcik,qikn->qpcn",
        lax.all_gather(antisym, "col", axis=3, tiled=True),
        chosen,
        precision=lax.Precision.HIGHEST,
    )
    chosen = rows_panel
    summed = lax.psum_scatter(
        jnp.einsum("qca,qpcn->apn", chosen, contracted, precision=lax.Precision.HIGHEST),
        "row",
        scatter_dimension=0,
        tiled=True,
    )
    pairs_out = summed.shape[1]
    result = (
        (0.5 * summed).reshape(local_rows, pairs_out, tile_count, sub_width).transpose(1, 0, 2, 3)
    )
    return result.reshape(pairs_out, 1, 1, local_rows * tile_count * sub_width)


def solution(mesh):
    placed = (P(None, "row", "col", None), P("occ", "row", "col", None), P(), P(), P(), P())
    return jax.shard_map(
        per_device,
        mesh=mesh,
        in_specs=placed,
        out_specs=P("occ", "row", "col", None),
        check_vma=False,
    )
```

profile of v0, /device:TPU:5, one launch (start us, length us, event | category | flops | bytes accessed | tf_op | source)
XLA Modules:
  0.0 1035.4 jit_solution(3370676249435527496)
XLA Ops:
  6.5 0.0 copy-start.2
  6.5 0.0 all-gather.3.cloned.1.call-start
  6.6 1.0 select_reduce_fusion
  7.6 0.1 copy.55
  7.7 0.7 select_reduce_fusion.1
  8.4 0.8 copy.53
  9.2 1.0 convolution_compare_fusion
  10.2 0.4 copy.54
  10.7 2.2 reduce
  12.9 8.7 reshape.130
  21.6 0.2 broadcast_xor_fusion
  21.8 0.0 copy-done.2
  21.8 0.1 dynamic_slice.6
  21.9 6.1 and_select_fusion
  28.0 4.9 copy.56
  32.9 19.2 %all_gather.12 = f32[16,88,16,11]{1,2,3,0:T(8,128)S(1)} all-gather(f32[8,88,16,11]{1,2,3,0:T(8,128)S(1)} %copy.56), channel_id=1, replica_groups=mesh['row'=16,'col'=8,'occ'=2] {'occ'}, dimensions={0}, use_global_device_ids=true | all-gather | bytes 1486848 | tf_op jit(solution)/shard_map/all_gather | solution.py:52
  52.1 1.3 copy.57
  53.4 0.0 all-gather.3.cloned.1.call-update
  53.4 0.0 all-gather.5.cloned.1.call-start
  53.5 4.9 copy.59
  58.4 0.0 copy-start.1
  58.4 0.0 copy-start.3
  58.5 0.0 all-gather.5.cloned.1.call-update
  58.5 0.0 reduce-scatter.4.cloned.1.call-start
  58.5 0.8 copy-done.1
  59.3 0.4 reduce.1
  59.7 2.5 reshape.133
  62.2 0.0 copy-done.3
  62.2 0.6 dynamic-slice
  62.8 1.8 dynamic-slice_select_fusion
  64.7 0.9 copy.62
  65.6 0.7 reshape.146
  66.3 11.2 %all_to_all.20 = f32[16,1,968]{2,1,0:T(1,128)S(1)} all-to-all(f32[16,1,968]{2,1,0:T(1,128)S(1)} %reshape.146), channel_id=1, replica_groups=mesh['row'=16,'col'=8,'occ'=2] {'row'}, dimensions={0} | all-to-all | bytes 123904 | tf_op jit(solution)/shard_map/all_to_all | solution.py:57
  77.5 0.5 broadcast.129
  78.0 0.8 reduce.2
  78.8 0.3 reshape.147
  79.1 0.9 copy.63
  80.0 1.9 reduce.3
  81.9 0.3 reshape.148
  82.2 16.3 %all_to_all.21 = f32[8,1,1936]{2,1,0:T(1,128)S(1)} all-to-all(f32[8,1,1936]{2,1,0:T(1,128)S(1)} %reshape.148), channel_id=1, replica_groups=mesh['row'=16,'col'=8,'occ'=2] {'col'}, dimensions={0} | all-to-all | bytes 123904 | tf_op jit(solution)/shard_map/all_to_all | solution.py:56
  98.5 0.8 reduce.4
  99.3 0.5 reshape.149
  99.9 0.1 bitcast_bitcast_fusion
  100.0 0.7 copy.73
  100.7 0.1 sub.17
  100.8 0.3 copy.66
  101.1 24.9 %all_gather.15 = f32[1,88,16,88]{1,2,0,3:T(8,128)S(1)} all-gather(f32[1,88,16,11]{1,2,0,3:T(8,128)S(1)} %copy.66), channel_id=1, replica_groups=mesh['row'=16,'col'=8,'occ'=2] {'col'}, dimensions={3}, use_global_device_ids=true | all-gather | bytes 557568 | tf_op jit(solution)/shard_map/all_gather | solution.py:73
  126.0 0.3 copy.67
  126.4 62.8 %all-gather.3.cloned.1.call-done = f32[16,88,16,88]{1,2,0,3:T(8,128)} async-done(((f32[16,88,16,11]{1,2,0,3:T(8,128)}), f32[16,88,16,88]{1,2,0,3:T(8,128)}) %all-gather.3.cloned.1.call-update) | async-done | bytes 7929872 | tf_op jit(solution)/shard_map/all_gather | solution.py:67
  189.2 14.1 %copy.58 = f32[16,88,16,88]{3,2,1,0:T(8,128)} copy(f32[16,88,16,88]{1,2,0,3:T(8,128)} %all-gather.3.cloned.1.call-done) | data formatting | bytes 15859712 | tf_op jit(solution)/shard_map/all_gather | solution.py:67
  203.3 13.0 %reshape.131 = f32[16,88,1408]{2,1,0:T(8,128)} reshape(f32[16,88,16,88]{3,2,1,0:T(8,128)} %copy.58) | data formatting | bytes 15859712 | tf_op jit(solution)/shard_map/reshape | solution.py:67
  216.3 585.6 %all-gather.5.cloned.1.call-done = f32[16,1408,16,11]{2,0,3,1:T(8,128)} async-done(((f32[16,88,16,11]{2,0,3,1:T(8,128)}), f32[16,1408,16,11]{2,0,3,1:T(8,128)}) %all-gather.5.cloned.1.call-update) | async-done | bytes 15859728 | tf_op jit(solution)/shard_map/all_gather | solution.py:65
  801.9 80.9 %copy.60 = f32[16,1408,16,11]{1,0,3,2:T(8,128)} copy(f32[16,1408,16,11]{2,0,3,1:T(8,128)} %all-gather.5.cloned.1.call-done) | data formatting | bytes 31719424 | tf_op jit(solution)/shard_map/all_gather | solution.py:65
  882.8 27.3 %reshape.132 = f32[16,16,88,176]{2,1,0,3:T(8,128)} reshape(f32[16,1408,16,11]{1,0,3,2:T(8,128)} %copy.60) | data formatting | bytes 31719424 | tf_op jit(solution)/shard_map/reshape | solution.py:66
  910.1 0.0 copy-start
  910.1 35.5 %fusion.2 = f32[16,88,176]{1,2,0:T(8,128)S(1)} fusion(f32[16,16,88,176]{2,1,0,3:T(8,128)} %reshape.132, f32[1,88,16,88]{3,1,2,0:T(8,128)S(1)} %copy.67), kind=kOutput, calls=%fused_computation.4 | convolution fusion | flops 4186963968 | bytes 17346560 | tf_op jit(solution)/shard_map/pcik,qikn->qpcn/dot_general | solution.py:71
  945.7 0.0 copy-done
  945.7 20.0 %convolution_bitcast_fusion = f32[1408,176]{1,0:T(8,128)} fusion(f32[16,88,1408]{2,1,0:T(8,128)S(1)} %copy-done, f32[16,88,176]{1,2,0:T(8,128)S(1)} %fusion.2), kind=kOutput, calls=%fused_computation.3 | convolution fusion | flops 4186963968 | bytes 9912320 | tf_op jit(solution)/shard_map/qca,qpcn->apn/dot_general | solution.py:79
  965.7 0.0 reduce-scatter.4.cloned.1.call-update
  965.7 61.0 %reduce-scatter.4.cloned.1.call-done = f32[88,176]{1,0:T(8,128)} async-done(((f32[1408,176]{1,0:T(8,128)}), f32[88,176]{1,0:T(8,128)}) %reduce-scatter.4.cloned.1.call-update) | async-done | bytes 61968
  1026.7 1.0 copy.78
  1027.8 0.1 copy.69
  1027.8 0.8 reshape_transpose_reshape.3
  (4 shorter events, 0.0 us)
Async XLA Ops:
  6.5 15.2 %copy-start.2 = (s32[16]{0:T(128)S(1)}, s32[16]{0:T(128)}, u32[]{:S(2)}) copy-start(s32[16]{0:T(128)} %param.10) | copy-start | bytes 196
  6.5 182.6 %all-gather.3.cloned.1.call-start = ((), (), s32[]{:S(2)}) async-start(), calls=%async_computation.3 | async-start | bytes 12976128 | tf_op jit(solution)/shard_map/all_gather | solution.py:67
  53.4 748.4 %all-gather.5.cloned.1.call-start = ((), (), s32[]{:S(2)}) async-start(), calls=%async_computation.4 | async-start | bytes 134807552 | tf_op jit(solution)/shard_map/all_gather | solution.py:65
  58.4 0.9 copy-start.1
  58.4 3.8 copy-start.3
  58.5 968.3 %reduce-scatter.4.cloned.1.call-start = ((), (), s32[]{:S(2)}) async-start(), calls=%async_computation.5 | async-start | bytes 1531904
  910.1 35.5 %copy-start = (f32[16,88,1408]{2,1,0:T(8,128)S(1)}, f32[16,88,1408]{2,1,0:T(8,128)}, u32[]{:S(2)}) copy-start(f32[16,88,1408]{2,1,0:T(8,128)} %reshape.131) | copy-start | bytes 23789572
Sparse Core Ops, SparseCore 0:
  53.6 135.5 all-gather.2
  191.0 610.8 all-gather.4
  965.8 60.8 reduce-scatter.3
where the time goes:
time: 1050 us; the launch traced here: 1040 us
  waiting for transfers between devices  710 us (68%)
  local copies, waits for them, and re-layouts  168 us (16%)
  blocking collectives  71.5 us (7%)
  matrix products  56.5 us (5%)
  other arithmetic  16.1 us (2%)
  between operations  13.5 us (1%)
    all_gather x1, waiting for transfers between devices, per_device(): columns = lax.all_gather(factor, 'row', axis=1, tiled=True)  586 us
    all_gather x1, local copies, waits for them, and re-layouts, per_device(): columns = lax.all_gather(factor, 'row', axis=1, tiled=True)  80.9 us
    all_gather x1, waiting for transfers between devices, per_device(): lax.all_gather(factor, 'col', axis=3, tiled=True)  62.8 us
    unnamed x4, waiting for transfers between devices  61.1 us
    dot_general x1, matrix products, per_device(): jnp.einsum('pcik,qikn->qpcn', lax.all_gather(antisym, 'col', axis=3, tile...  35.5 us
    reshape x1, local copies, waits for them, and re-layouts, per_device(): columns.reshape(aux_count, tile_count, local_rows, tile_count * sub_width)  27.3 us
    all_gather x1, blocking collectives, per_device(): lax.all_gather(antisym, 'col', axis=3, tiled=True)  24.9 us
  transfers between devices with their start and end apart: 3, of which 3 were waited for; matrix products, arithmetic and copies ran while one was open for 5% of the time, Pallas kernels for 0%

commit v1 on v0

--- a/solution.py
+++ b/solution.py
@@ -1,10 +1,552 @@
+import functools
+
 import jax
 import jax.numpy as jnp
+import numpy as np
 from jax import lax
+from jax.experimental import pallas as pl
+from jax.experimental.pallas import tpu as pltpu
 from jax.sharding import PartitionSpec as P
 
 VIRTUALS = 1408
 BLOCK_WIDTH = 64
+BLOCKS = 22
+LABELS = 8
+ROWS, COLS = 16, 8
+TILE = 88
+WIDE = 176
+STRIPS = 11
+SLOTS = 64
+HALF = 48
+NAT = 512
+MESH = pl.DeviceIdType.MESH
+MIB = 1 << 20
+F32, BF16, I32 = jnp.float32, jnp.bfloat16, jnp.int32
+
+
+def coords():
+    return lax.axis_index("row"), lax.axis_index("col"), lax.axis_index("occ")
+
+
+def iota(shape, dim):
+    return lax.broadcasted_iota(I32, shape, dim)
+
+
+def div11(v):
+    return (v * 5958) >> 16
+
+
+def split(x):
+    hi = x.astype(BF16)
+    return hi, (x - hi.astype(F32)).astype(BF16)
+
+
+def dot_nn(a, b):
+    return lax.dot_general(a, b, (((1,), (0,)), ((), ())), preferred_element_type=F32)
+
+
+def dot_nt(a, b):
+    return lax.dot_general(a, b, (((1,), (1,)), ((), ())), preferred_element_type=F32)
+
+
+def cols_before(n, s):
+    return (n // TILE) * STRIPS + jnp.clip(n % TILE - STRIPS * s, 0, STRIPS)
+
+
+def column_facts(virt, s, shape):
+    w = iota(shape, 1)
+    d = w + 77 * div11(w) + STRIPS * s
+    block = d >> 6
+    before = [cols_before(BLOCK_WIDTH * b, s) for b in range(BLOCKS + 1)]
+    labels = [virt[b] for b in range(BLOCKS)]
+    label = jnp.zeros(shape, I32)
+    rank = w
+    for b in range(BLOCKS):
+        base = -before[b]
+        for e in range(b):
+            base = base + jnp.where(labels[e] == labels[b], before[e + 1] - before[e], 0)
+        here = block == b
+        label = jnp.where(here, labels[b], label)
+        rank = jnp.where(here, w + base, rank)
+    return d, block, label, rank
+
+
+def row_label(virt, block, first):
+    label = virt[first]
+    for k in (1, 2):
+        label = jnp.where(block == first + k, virt[jnp.minimum(first + k, BLOCKS - 1)], label)
+    return label
+
+
+def pack_kernel(virt, pair, aux, pat, a_ref, b_ref, ac_ref, bc_ref, d_ref):
+    r, s, o = coords()
+    first = (STRIPS * r) >> 3
+    d, block, label, rank = column_facts(virt, s, (1, WIDE))
+    sel = jnp.where((iota((128, WIDE), 0) & (SLOTS - 1)) == rank, 1.0, 0.0).astype(BF16)
+    screens = []
+    for k in range(3):
+        x = jnp.minimum(first + k, BLOCKS - 1)
+        flag = jnp.zeros((1, WIDE), I32)
+        for b in range(BLOCKS):
+            flag = jnp.where(block == b, pat[x, b] * pat[b, x], flag)
+        screens.append(flag)
+
+    row = iota((TILE, 1), 0)
+    q = div11(row)
+    row_block = (STRIPS * r + row - STRIPS * q) >> 3
+    target = row_label(virt, row_block, first)
+    aux_row = jnp.zeros((TILE, 1), I32)
+    for k in range(8):
+        aux_row = jnp.where(q == k, aux[8 * o + k], aux_row)
+    target = target ^ aux_row
+    screen = jnp.where(
+        row_block == first, screens[0], jnp.where(row_block == first + 1, screens[1], screens[2])
+    )
+    keep_b = jnp.logical_and(label == target, screen > 0)
+
+    row = iota((2 * STRIPS, 1), 0)
+    p = jnp.where(row >= STRIPS, 1, 0)
+    row_block = (STRIPS * r + row - STRIPS * p) >> 3
+    keep_a = label == (row_label(virt, row_block, first) ^ jnp.where(p == 1, pair[1], pair[0]))
+
+    for src, count, base, keep in ((b_ref, 8, 0, keep_b), (a_ref, 2, 8 * TILE, keep_a)):
+        n = count * STRIPS
+        lines = [src[pl.ds(k, n, stride=STRIPS), :] for k in range(STRIPS)]
+        for v in range(8):
+            start = WIDE * v
+            low, off = start // 128, start % 128
+            last = (start + WIDE - 1) // 128
+            tile = jnp.concatenate(lines[low : last + 1], axis=1)[:, off : off + WIDE]
+            hi, lo = split(jnp.where(keep, tile, 0.0))
+            d_ref[pl.ds(base + v, n, stride=8), :] = dot_nt(hi, sel) + dot_nt(lo, sel)
+    d_ref[10 * TILE : 10 * TILE + 8, :] = jnp.zeros((8, 128), F32)
+    left = iota((HALF, 128), 1) < SLOTS
+    for k in range(10):
+        top, bottom = d_ref[pl.ds(TILE * k, HALF), :], d_ref[pl.ds(TILE * k + HALF, HALF), :]
+        if k < 8:
+            bc_ref[k] = jnp.where(left, top, bottom)
+        else:
+            ac_ref[k - 8] = jnp.where(left, top, bottom)
+
+
+def gather_kernel(ac_ref, bc_ref, aa_ref, sa_ref, send, recv, near):
+    r, s, o = coords()
+    c, x, y = r % 2, (r // 2) % 4, r // 8
+
+    def at(cc, xx, yy, ss):
+        return (yy * 8 + xx * 2 + cc, ss, o)
+
+    zs = [(at(c, x, y, (s + k) % 8)) for k in range(1, 8)]
+    xs = [(at(c, (x + k) % 4, y, s)) for k in range(1, 4)]
+    ynear = at(c, x, 1 - y, s)
+    sibling = at(1 - c, x, y, s)
+    barrier = pltpu.get_barrier_semaphore()
+    for peer in zs + xs + [ynear, sibling]:
+        pl.semaphore_signal(barrier, inc=1, device_id=peer, device_id_type=MESH)
+    pl.semaphore_wait(barrier, 12)
+
+    copies = []
+
+    def put(src, dst, peer, n):
+        copy = pltpu.make_async_remote_copy(
+            src_ref=src,
+            dst_ref=dst,
+            send_sem=send.at[n],
+            recv_sem=recv.at[n],
+            device_id=peer,
+            device_id_type=MESH,
+        )
+        copy.start()
+        copies.append(copy)
+        return copy
+
+    def arrived(ref, n):
+        pltpu.make_async_remote_copy(
+            src_ref=ref,
+            dst_ref=ref,
+            send_sem=send.at[n],
+            recv_sem=recv.at[n],
+            device_id=sibling,
+            device_id_type=MESH,
+        ).wait_recv()
+
+    own_a = pltpu.make_async_copy(ac_ref.at[y], aa_ref.at[c, x, y, s], near.at[0])
+    own_s = pltpu.make_async_copy(bc_ref.at[s], sa_ref.at[c, x, y, s], near.at[1])
+    put(ac_ref.at[1 - y], aa_ref.at[c, x, y, s], ynear, 7)
+    for k in range(1, 8):
+        put(bc_ref.at[(s + k) % 8], sa_ref.at[c, x, y, s], zs[k - 1], k - 1)
+    own_a.start()
+    own_s.start()
+    own_a.wait()
+    arrived(aa_ref.at[c, x, 1 - y, s], 7)
+    for k in range(1, 4):
+        put(aa_ref.at[c, x, :, s], aa_ref.at[c, x, :, s], xs[k - 1], 7 + k)
+    own_s.wait()
+    for k in range(1, 8):
+        arrived(sa_ref.at[c, x, y, (s - k + 8) % 8], k - 1)
+    put(sa_ref.at[c, x, y], sa_ref.at[c, x, y], ynear, 18)
+    for k in range(1, 4):
+        arrived(aa_ref.at[c, (x - k + 4) % 4, :, s], 7 + k)
+    for k in range(1, 8):
+        put(aa_ref.at[c, :, :, s], aa_ref.at[c, :, :, s], zs[k - 1], 10 + k)
+    put(aa_ref.at[c, :, :, s], aa_ref.at[c, :, :, s], sibling, 26)
+    arrived(sa_ref.at[c, x, 1 - y], 18)
+    for k in range(1, 4):
+        put(sa_ref.at[c, x], sa_ref.at[c, x], xs[k - 1], 18 + k)
+    put(sa_ref.at[c, x], sa_ref.at[c, x], sibling, 22)
+    for k in range(1, 4):
+        xk = (x - k + 4) % 4
+        arrived(sa_ref.at[c, xk], 18 + k)
+        put(sa_ref.at[c, xk], sa_ref.at[c, xk], sibling, 22 + k)
+    for k in range(1, 8):
+        sk = (s - k + 8) % 8
+        arrived(aa_ref.at[c, :, :, sk], 10 + k)
+        put(aa_ref.at[c, :, :, sk], aa_ref.at[c, :, :, sk], sibling, 26 + k)
+    arrived(sa_ref.at[1 - c, x], 22)
+    for k in range(1, 4):
+        arrived(sa_ref.at[1 - c, (x - k + 4) % 4], 22 + k)
+    arrived(aa_ref.at[1 - c, :, :, s], 26)
+    for k in range(1, 8):
+        arrived(aa_ref.at[1 - c, :, :, (s - k + 8) % 8], 26 + k)
+    for copy in copies:
+        copy.wait_send()
+
+
+def product_kernel(
+    virt, pair, aux, aa_ref, sa_ref, z_ref, a2, s2, v1, v2, zs, whi, wlo, lists, counts
+):
+    r, s, o = coords()
+    core, x_me, pair_me = r % 2, (r // 2) % 4, r // 8
+    h = aux[8 * o + s]
+    hp = h ^ pair[pair_me]
+    left = iota((HALF, 128), 1) < SLOTS
+
+    def unpack(k, _):
+        c, x, y = k % 2, (k // 2) % 4, k // 8
+        base = pl.multiple_of(k * TILE, 8)
+        for src, dst in ((sa_ref, s2), (aa_ref, a2)):
+            for j in range(4):
+                even, odd = src[c, x, y, 2 * j], src[c, x, y, 2 * j + 1]
+                top = jnp.where(left, even, pltpu.roll(odd, SLOTS, 1))
+                bottom = jnp.where(left, pltpu.roll(even, SLOTS, 1), odd)
+                dst[pl.ds(base, HALF), pl.ds(128 * j, 128)] = top
+                dst[pl.ds(base + HALF, TILE - HALF), pl.ds(128 * j, 128)] = bottom[: TILE - HALF]
+        return 0
+
+    lax.fori_loop(0, ROWS, unpack, 0)
+    for ref in (s2, a2):
+        ref[VIRTUALS:, :] = jnp.zeros((BLOCK_WIDTH, NAT), F32)
+
+    for g in range(LABELS):
+        counts[g] = 0
+        for j in range(8):
+            lists[8 * g + j] = BLOCKS
+    places = []
+    for b in range(BLOCKS):
+        g = virt[b]
+        n = counts[g]
+        lists[8 * g + jnp.minimum(n, 7)] = b
+        counts[g] = n + 1
+        places.append(n)
+
+    group = iota((8, 1), 0)
+    d, block, label, rank = column_facts(virt, group, (8, WIDE))
+    place = jnp.zeros((8, WIDE), I32)
+    for b in range(BLOCKS):
+        place = jnp.where(block == b, places[b], place)
+    natural = place * BLOCK_WIDTH + (d & (BLOCK_WIDTH - 1))
+
+    tiles = (2 * x_me + core, 8 + 2 * x_me + core)
+    bases = [pl.multiple_of(t * TILE, 8) for t in tiles]
+    firsts = [(STRIPS * t) >> 3 for t in tiles]
+    row = iota((TILE, 1), 0)
+    row_blocks = [(t * TILE + row) >> 6 for t in tiles]
+    labels = jnp.concatenate([row_label(virt, b, f) for b, f in zip(row_blocks, firsts)], axis=0)
+
+    def to_natural(x, target):
+        hi, lo = split(x)
+        both = jnp.concatenate([hi, lo], axis=0)
+        target = jnp.concatenate([target, target], axis=0)
+        total = jnp.zeros((2 * WIDE, NAT), F32)
+        for k in range(8):
+            j = k // 2
+            spread = jnp.where(
+                iota((128, WIDE), 0) == rank[k : k + 1] + SLOTS * (k % 2), 1.0, 0.0
+            ).astype(BF16)
+            dense = dot_nn(both[:, 128 * j : 128 * j + 128], spread)
+            dense = jnp.where(label[k : k + 1] == target, dense, 0.0).astype(BF16)
+            pick = jnp.where(iota((NAT, WIDE), 0) == natural[k : k + 1], 1.0, 0.0).astype(BF16)
+            total = total + dot_nt(dense, pick)
+        return total[:WIDE] + total[WIDE:]
+
+    own = [s2[pl.ds(b, TILE), :] for b in bases]
+    own_natural = to_natural(jnp.concatenate(own, axis=0), labels ^ h)
+
+    def load_rows(src, g, half):
+        for j in range(4):
+            b = lists[8 * g + 4 * half + j]
+            hi, lo = split(src[pl.ds(pl.multiple_of(b * BLOCK_WIDTH, BLOCK_WIDTH), BLOCK_WIDTH), :])
+            whi[pl.ds(BLOCK_WIDTH * j, BLOCK_WIDTH), :] = hi
+            wlo[pl.ds(BLOCK_WIDTH * j, BLOCK_WIDTH), :] = lo
+
+    def dot3(dot, a):
+        hi, lo = split(a)
+        return dot(hi, whi[...]) + dot(lo, whi[...]) + dot(hi, wlo[...])
+
+    v1[...] = jnp.zeros_like(v1)
+    v2[...] = jnp.zeros_like(v2)
+    zs[...] = jnp.zeros_like(zs)
+    for t in range(2):
+        last = (STRIPS * tiles[t] + STRIPS - 1) >> 3
+
+        def first_product(x, _, t=t):
+            g1 = virt[x] ^ h
+            g2 = virt[x] ^ hp
+            here = row_blocks[t] == x
+            mine = jnp.where(here, own[t], 0.0)
+            mine_natural = jnp.where(here, own_natural[TILE * t : TILE * t + TILE], 0.0)
+            for half in range(2):
+                part = slice(256 * half, 256 * half + 256)
+
+                @pl.when(counts[g1] > 4 * half)
+                def _():
+                    load_rows(a2, g1, half)
+                    v2[t] += dot3(dot_nn, mine_natural[:, part])
+
+                @pl.when(counts[g2] > 4 * half)
+                def _():
+                    load_rows(a2, g2, half)
+                    v1[t, :, part] += dot3(dot_nt, mine)
+
+            return 0
+
+        lax.fori_loop(firsts[t], last + 1, first_product, 0)
+
+    turned = to_natural(jnp.concatenate([v2[0], v2[1]], axis=0), labels ^ hp)
+    for t in range(2):
+        last = (STRIPS * tiles[t] + STRIPS - 1) >> 3
+        y = turned[TILE * t : TILE * t + TILE] - v1[t]
+
+        def second_product(x, _, t=t, y=y):
+            g2 = virt[x] ^ hp
+            mine = jnp.where(row_blocks[t] == x, y, 0.0)
+            for half in range(2):
+
+                @pl.when(counts[g2] > 4 * half)
+                def _():
+                    load_rows(s2, g2, half)
+                    zs[t, :TILE] += dot3(dot_nn, mine[:, 256 * half : 256 * half + 256])
+
+            return 0
+
+        lax.fori_loop(firsts[t], last + 1, second_product, 0)
+
+    for t in range(2):
+        for k in range(8):
+            j = k // 2
+            top = zs[t, 0:HALF, pl.ds(128 * j, 128)]
+            bottom = zs[t, HALF : 2 * HALF, pl.ds(128 * j, 128)]
+            if k % 2 == 0:
+                z_ref[t, k] = jnp.where(left, top, pltpu.roll(bottom, SLOTS, 1))
+            else:
+                z_ref[t, k] = jnp.where(left, pltpu.roll(top, SLOTS, 1), bottom)
+
+
+def scatter_kernel(z_ref, out_ref, send, recv, near):
+    r, s, o = coords()
+    y, rest = r // 8, r % 8
+    alone = jnp.where(y == o, 1, 0)
+    barrier = pltpu.get_barrier_semaphore()
+
+    def greet(e, k):
+        pl.semaphore_signal(
+            barrier, inc=1, device_id=(o * 8 + rest, (s + k) % 8, e), device_id_type=MESH
+        )
+
+    def describe(e, k):
+        return pltpu.make_async_remote_copy(
+            src_ref=z_ref.at[e, (s + k) % 8],
+            dst_ref=out_ref.at[o, s],
+            send_sem=send.at[8 * e + k],
+            recv_sem=recv.at[8 * o + k],
+            device_id=(e * 8 + rest, (s + k) % 8, y),
+            device_id_type=MESH,
+        )
+
+    def sender(e, k):
+        describe(e, k).start()
+
+    def receive(e, k):
+        spot = out_ref.at[e, (s - k + 8) % 8]
+        pltpu.make_async_remote_copy(
+            src_ref=spot,
+            dst_ref=spot,
+            send_sem=send.at[0],
+            recv_sem=recv.at[8 * e + k],
+            device_id=(o * 8 + rest, (s + 1) % 8, e),
+            device_id_type=MESH,
+        ).wait_recv()
+
+    def finish(e, k):
+        describe(e, k).wait_send()
+
+    def each(fn, mine):
+        for k in list(range(1, 8)) + [0]:
+            for e in range(2):
+                if k:
+                    fn(e, k)
+                else:
+                    pl.when(jnp.logical_or(y != o, mine != e))(functools.partial(fn, e, k))
+
+    each(greet, o)
+    pl.semaphore_wait(barrier, 16 - alone)
+    each(sender, y)
+
+    @pl.when(y == o)
+    def _():
+        copy = pltpu.make_async_copy(z_ref.at[y, s], out_ref.at[o, s], near.at[0])
+        copy.start()
+        copy.wait()
+
+    each(receive, o)
+    each(finish, y)
+
+
+def finish_kernel(virt, pair, parts_ref, out_ref, low_ref, high_ref):
+    r, s, o = coords()
+    first = (STRIPS * r) >> 3
+    d, block, label, rank = column_facts(virt, s, (1, WIDE))
+    total = parts_ref[0, 0]
+    for k in range(1, 16):
+        total = total + parts_ref[k // 8, k % 8]
+    hi, lo = split(0.5 * total)
+    row = iota((HALF, 1), 0)
+    for half in range(2):
+        spread = jnp.where(iota((128, WIDE), 0) == rank + SLOTS * half, 1.0, 0.0).astype(BF16)
+        dense = dot_nn(hi, spread) + dot_nn(lo, spread)
+        row_block = (TILE * r + HALF * half + row) >> 6
+        keep = label == (row_label(virt, row_block, first) ^ pair[o])
+        dense = jnp.where(keep, dense, 0.0)
+        low_ref[HALF * half : HALF * half + HALF, :] = dense[:, :128]
+        high_ref[HALF * half : HALF * half + HALF, : WIDE - 128] = dense[:, 128:]
+    lines = []
+    for v in range(8):
+        low, high = low_ref[pl.ds(v, STRIPS, stride=8), :], high_ref[pl.ds(v, STRIPS, stride=8), :]
+        lines.append(jnp.concatenate([low, high[:, : WIDE - 128]], axis=1))
+    for k in range(STRIPS):
+        v, w = (128 * k) // WIDE, (128 * k) % WIDE
+        piece = lines[v][:, w : min(WIDE, w + 128)]
+        if w + 128 > WIDE:
+            piece = jnp.concatenate([piece, lines[v + 1][:, : w + 128 - WIDE]], axis=1)
+        out_ref[pl.ds(k, STRIPS, stride=STRIPS), :] = piece
+
+
+def smem(n):
+    return [pl.BlockSpec(memory_space=pltpu.SMEM)] * n
+
+
+def vmem(n):
+    return [pl.BlockSpec(memory_space=pltpu.VMEM)] * n
+
+
+def anywhere(n):
+    return [pl.BlockSpec(memory_space=pl.ANY)] * n
+
+
+def shape(*dims):
+    return jax.ShapeDtypeStruct(dims, F32)
+
+
+def run_pack(virt, pair, aux, pat, a, b):
+    return pl.pallas_call(
+        pack_kernel,
+        out_shape=(shape(2, HALF, 128), shape(8, HALF, 128)),
+        in_specs=smem(4) + vmem(2),
+        out_specs=tuple(vmem(2)),
+        scratch_shapes=[pltpu.VMEM((10 * TILE + 8, 128), F32)],
+        compiler_params=pltpu.CompilerParams(vmem_limit_bytes=32 * MIB),
+    )(virt, pair, aux, pat, a, b)
+
+
+def run_gather(ac, bc):
+    full = shape(2, 4, 2, 8, HALF, 128)
+    return pl.pallas_call(
+        gather_kernel,
+        out_shape=(full, full),
+        in_specs=anywhere(2),
+        out_specs=tuple(anywhere(2)),
+        scratch_shapes=[
+            pltpu.SemaphoreType.DMA((34,)),
+            pltpu.SemaphoreType.DMA((34,)),
+            pltpu.SemaphoreType.DMA((2,)),
+        ],
+        compiler_params=pltpu.CompilerParams(collective_id=0, has_side_effects=True),
+    )(ac, bc)
+
+
+def run_product(virt, pair, aux, aa, sa):
+    tall = pltpu.VMEM((VIRTUALS + BLOCK_WIDTH, NAT), F32)
+    return pl.pallas_call(
+        product_kernel,
+        out_shape=shape(2, 8, HALF, 128),
+        in_specs=smem(3) + vmem(2),
+        out_specs=vmem(1)[0],
+        scratch_shapes=[
+            tall,
+            tall,
+            pltpu.VMEM((2, TILE, NAT), F32),
+            pltpu.VMEM((2, TILE, NAT), F32),
+            pltpu.VMEM((2, 2 * HALF, NAT), F32),
+            pltpu.VMEM((256, NAT), BF16),
+            pltpu.VMEM((256, NAT), BF16),
+            pltpu.SMEM((64,), I32),
+            pltpu.SMEM((8,), I32),
+        ],
+        compiler_params=pltpu.CompilerParams(vmem_limit_bytes=48 * MIB),
+    )(virt, pair, aux, aa, sa)
+
+
+def run_scatter(z):
+    return pl.pallas_call(
+        scatter_kernel,
+        out_shape=shape(2, 8, HALF, 128),
+        in_specs=anywhere(1),
+        out_specs=anywhere(1)[0],
+        scratch_shapes=[
+            pltpu.SemaphoreType.DMA((16,)),
+            pltpu.SemaphoreType.DMA((16,)),
+            pltpu.SemaphoreType.DMA((1,)),
+        ],
+        compiler_params=pltpu.CompilerParams(collective_id=1, has_side_effects=True),
+    )(z)
+
+
+def run_finish(virt, pair, parts):
+    return pl.pallas_call(
+        finish_kernel,
+        out_shape=shape(121, 128),
+        in_specs=smem(2) + vmem(1),
+        out_specs=vmem(1)[0],
+        scratch_shapes=[pltpu.VMEM((2 * HALF, 128), F32)] * 2,
+        compiler_params=pltpu.CompilerParams(vmem_limit_bytes=32 * MIB),
+    )(virt, pair, parts)
+
+
+def packed_path(amplitudes, aux_factor, virt, pair, aux, pat):
+    ac, bc = run_pack(virt, pair, aux, pat, amplitudes.reshape(242, 128), aux_factor.reshape(968, 128))
+    aa, sa = run_gather(ac, bc)
+    z = run_product(virt, pair, aux, aa, sa)
+    out = run_finish(virt, pair, run_scatter(z))
+    return out.reshape(1, 1, 1, TILE * WIDE)
+
+
+def labels_fit(virt):
+    edges = np.arange(BLOCKS + 1)[:, None] * BLOCK_WIDTH
+    before = edges // TILE * STRIPS + np.clip(edges % TILE - STRIPS * np.arange(COLS), 0, STRIPS)
+    share = jnp.asarray(before[1:] - before[:-1], I32)
+    same = virt[:, None] == jnp.arange(LABELS, dtype=I32)
+    totals = jnp.sum(jnp.where(same[:, :, None], share[:, None, :], 0), axis=0)
+    return jnp.max(totals) <= SLOTS
 
 
 def block_onehot(indices, block_count):
@@ -15,7 +557,7 @@
     return jnp.sum(jnp.where(hot_table, virt_irrep, 0), axis=-1)
 
 
-def per_device(amplitudes, aux_factor, virt_irrep, pair_irrep, aux_irrep, block_pattern):
+def dense_path(amplitudes, aux_factor, virt_irrep, pair_irrep, aux_irrep, block_pattern):
     tile_count = lax.axis_size("row")
     col_count = lax.axis_size("col")
     local_rows = VIRTUALS // tile_count
@@ -88,6 +630,10 @@
     return result.reshape(pairs_out, 1, 1, local_rows * tile_count * sub_width)
 
 
+def per_device(*args):
+    return lax.cond(labels_fit(args[2]), packed_path, dense_path, *args)
+
+
 def solution(mesh):
     placed = (P(None, "row", "col", None), P("occ", "row", "col", None), P(), P(), P(), P())
     return jax.shard_map(

time: 1050 us -> 113 us (0.11); the launches traced: 1040 us -> 113 us
  waiting for transfers between devices: 710 us -> 0 us
  local copies, waits for them, and re-layouts: 168 us -> 5.67 us
  Pallas kernels: 0 us -> 89.6 us
  blocking collectives: 71.5 us -> 0 us
  matrix products: 56.5 us -> 0 us
  other arithmetic: 16.1 us -> 3.46 us
    all_gather x2 -> x0, waiting for transfers between devices: 648 us -> none  [the longest x1 586 us: per_device(): columns = lax.all_gather(factor, 'row', axis=1, tiled=True)]
    all_gather x5 -> x0, local copies, waits for them, and re-layouts: 102 us -> none  [the longest x1 80.9 us: per_device(): columns = lax.all_gather(factor, 'row', axis=1, tiled=True)]
    pallas_call x0 -> x5, Pallas kernels: none -> 89.6 us  [the longest x1 54.8 us: run_gather(): pl.pallas_call(gather_kernel, out_shape=(full, full), in_specs=anywhere(2...]
    unnamed x4 -> x0, waiting for transfers between devices: 61.1 us -> none
    dot_general x3 -> x0, matrix products: 56.5 us -> none  [the longest x1 35.5 us: per_device(): jnp.einsum('pcik,qikn->qpcn', lax.all_gather(antisym, 'col', axis=3, tile...]
    reshape x6 -> x2, local copies, waits for them, and re-layouts: 53.2 us -> 0.16 us  [the longest x1 0.1 us: packed_path(): amplitudes.reshape(242, 128)]
    all_gather x2 -> x0, blocking collectives: 44.1 us -> none  [the longest x1 24.9 us: per_device(): lax.all_gather(antisym, 'col', axis=3, tiled=True)]
    all_to_all x2 -> x0, blocking collectives: 27.5 us -> none  [the longest x1 16.3 us: per_device(): lax.all_to_all(lax.all_to_all(split_view, 'row', split_axis=3, concat_axi...]
  transfers between devices with their start and end apart: 3 -> 0, of which waited for: 3 -> 0; matrix products, arithmetic and copies ran while one was open for 5% -> 0% of each run, Pallas kernels for 0% -> 0%
where the time goes in v1:
time: 113 us
  Pallas kernels  89.6 us (79%)
  between operations  14 us (12%)
  local copies, waits for them, and re-layouts  5.67 us (5%)
  other arithmetic  3.46 us (3%)
    pallas_call x1, Pallas kernels, run_gather(): pl.pallas_call(gather_kernel, out_shape=(full, full), in_specs=anywhere(2...  54.8 us
    pallas_call x1, Pallas kernels, run_scatter(): pl.pallas_call(scatter_kernel, out_shape=shape(2, 8, HALF, 128), in_specs...  16.1 us
    pallas_call x1, Pallas kernels, run_product(): pl.pallas_call(product_kernel, out_shape=shape(2, 8, HALF, 128), in_specs...  15.1 us
    cond x14, local copies, waits for them, and re-layouts  4.89 us
    pallas_call x1, Pallas kernels, run_pack(): pl.pallas_call(pack_kernel, out_shape=(shape(2, HALF, 128), shape(8, HALF...  2.41 us

profile of v1, /device:TPU:5, one launch (start us, length us, event | category | flops | bytes accessed | tf_op | source)
XLA Modules:
  0.0 113.2 jit_solution(15658458396423385625)
XLA Ops:
  6.5 0.7 iota_compare_fusion.5
  7.2 0.9 select_reduce_fusion.2
  8.1 0.6 reduce_max.9
  9.4 96.3 %conditional.1 = (f32[1,1,1,15488]{3,2,1,0:T(1,128)S(1)}) conditional(s32[]{:T(128)} %convert_element_type.8, (s32[22,22]{1,0:T(8,128)}, s32[22]{0:T(128)}, s32[16]{0:T(128)}, f32[8,1,1,15488]{3,2,1,0:T(1,128)}, s32[2]{0:T(128)}, /*index=5*/f32[2,1,1,15488]{3,2,1,0:T(1,128)}) %tuple.11, (f32[2,1,1,15488]{3,2,1,0:T(1,128)}, ...), branch_computations={%region_2.6_spmd, %region_6.7_spmd} | conditional | flops 8375187456 | bytes 371862720 | solution.py:634
  9.6 0.0 copy-start.8
  9.6 0.0 copy-start.10
  9.7 1.3 %reduce = f32[2,15488]{1,0:T(2,128)S(1)} reduce(f32[2,1,1,15488]{3,2,1,0:T(1,128)} %get-tuple-element.103, f32[]{:T(128)} %constant.66), dimensions={1,2}, to_apply=%get-tuple-element.103.reduce_sub_computation | reduce | bytes 247812 | tf_op jit(solution)/shard_map
  10.9 0.1 reshape.161.a_ref
  11.0 2.4 %branch_1_fun.5 = (f32[2,48,128]{2,1,0:T(8,128)S(1)}, f32[8,48,128]{2,1,0:T(8,128)S(1)}) custom-call(s32[22]{0:T(128)} %get-tuple-element.38.virt, s32[2]{0:T(128)} %get-tuple-element.39.pair, s32[16]{0:T(128)} %get-tuple-element.40.aux, s32[22,22]{1,0:T(8,128)} %get-tuple-element.41.pat, f32[242,128]{1,0:T(8,128)S(1)} %reshape.161.a_ref, f32[968,128]{1,0:T(8,128)} %bitcast.65), custom_call_target="tpu_custom_call" | custom-call | tf_op jit(solution)/shard_map/cond/branch_1_fun/pallas_call | solution.py:461
  13.4 0.0 copy-start.3
  13.5 0.7 copy-done.3
  14.1 0.0 copy-start.4
  14.1 0.6 copy-done.4
  14.7 54.8 %branch_1_fun.6 = (f32[2,4,2,8,48,128]{5,4,3,2,1,0:T(8,128)}, f32[2,4,2,8,48,128]{5,4,3,2,1,0:T(8,128)}) custom-call(f32[2,48,128]{2,1,0:T(8,128)} %copy-done.4, f32[8,48,128]{2,1,0:T(8,128)} %copy-done.3), custom_call_target="tpu_custom_call" | custom-call | tf_op jit(solution)/shard_map/cond/branch_1_fun/pallas_call | solution.py:473
  69.6 0.0 copy-start
  69.6 1.9 %copy-done = f32[2,4,2,8,48,128]{5,4,3,2,1,0:T(8,128)S(1)} copy-done((f32[2,4,2,8,48,128]{5,4,3,2,1,0:T(8,128)S(1)}, f32[2,4,2,8,48,128]{5,4,3,2,1,0:T(8,128)}, u32[]{:S(2)}) %copy-start) | copy-done | bytes 3145752 | tf_op jit(solution)/shard_map/cond
  71.5 15.1 %branch_1_fun.7.z_ref = f32[2,8,48,128]{3,2,1,0:T(8,128)S(1)} custom-call(s32[22]{0:T(128)} %get-tuple-element.38.virt, s32[2]{0:T(128)} %get-tuple-element.39.pair, s32[16]{0:T(128)} %get-tuple-element.40.aux, f32[2,4,2,8,48,128]{5,4,3,2,1,0:T(8,128)S(1)} %copy-done, f32[2,4,2,8,48,128]{5,4,3,2,1,0:T(8,128)} %get-tuple-element.47.sa_ref), custom_call_target="tpu_custom_call" | custom-call | tf_op jit(solution)/shard_map/cond/branch_1_fun/pallas_call | solution.py:489
  86.6 0.0 copy-start.1
  86.6 0.7 copy-done.1
  87.3 16.1 %branch_1_fun.8.parts_ref = f32[2,8,48,128]{3,2,1,0:T(8,128)} custom-call(f32[2,8,48,128]{3,2,1,0:T(8,128)} %copy-done.1), custom_call_target="tpu_custom_call" | custom-call | tf_op jit(solution)/shard_map/cond/branch_1_fun/pallas_call | solution.py:510
  103.4 0.0 copy-done.8
  103.4 0.0 copy-done.10
  103.4 0.0 copy-start.2
  103.4 1.0 copy-done.2
  104.4 1.2 %branch_1_fun.9 = f32[121,128]{1,0:T(8,128)S(1)} custom-call(s32[22]{0:T(128)S(1)} %copy-done.8, s32[2]{0:T(128)S(1)} %copy-done.10, f32[2,8,48,128]{3,2,1,0:T(8,128)S(1)} %copy-done.2), custom_call_target="tpu_custom_call" | custom-call | tf_op jit(solution)/shard_map/cond/branch_1_fun/pallas_call | solution.py:525
  105.6 0.1 reshape.163
  105.7 0.0 copy-start.7
  105.7 0.6 copy-done.7
Async XLA Ops:
  9.6 93.8 %copy-start.8 = (s32[22]{0:T(128)S(1)}, s32[22]{0:T(128)}, u32[]{:S(2)}) copy-start(s32[22]{0:T(128)} %get-tuple-element.38.virt) | copy-start | bytes 268 | tf_op jit(solution)/shard_map/cond
  9.6 93.8 %copy-start.10 = (s32[2]{0:T(128)S(1)}, s32[2]{0:T(128)}, u32[]{:S(2)}) copy-start(s32[2]{0:T(128)} %get-tuple-element.39.pair) | copy-start | bytes 28 | tf_op jit(solution)/shard_map/cond
  13.4 0.7 copy-start.3
  14.1 0.6 copy-start.4
  69.6 1.9 %copy-start = (f32[2,4,2,8,48,128]{5,4,3,2,1,0:T(8,128)S(1)}, f32[2,4,2,8,48,128]{5,4,3,2,1,0:T(8,128)}, u32[]{:S(2)}) copy-start(f32[2,4,2,8,48,128]{5,4,3,2,1,0:T(8,128)} %get-tuple-element.46.aa_ref) | copy-start | bytes 9437188 | tf_op jit(solution)/shard_map/cond
  86.6 0.7 copy-start.1
  103.4 1.0 copy-start.2
  105.7 0.6 copy-start.7

commit v2 on v1

v2 whole, which is shorter than its diff:
```python
import functools

import jax
import jax.numpy as jnp
import numpy as np
from jax import lax
from jax.experimental import pallas as pl
from jax.experimental.pallas import tpu as pltpu
from jax.sharding import PartitionSpec as P

VIRTUALS = 1408
BLOCK_WIDTH = 64
BLOCKS = 22
LABELS = 8
ROWS, COLS = 16, 8
TILE = 88
WIDE = 176
STRIPS = 11
SLOTS = 64
HALF = 48
MESH = pl.DeviceIdType.MESH
MIB = 1 << 20
F32, BF16, I32 = jnp.float32, jnp.bfloat16, jnp.int32


def coords():
    return lax.axis_index("row"), lax.axis_index("col"), lax.axis_index("occ")


def iota(shape, dim):
    return lax.broadcasted_iota(I32, shape, dim)


def div11(v):
    return (v * 5958) >> 16


def split(x):
    hi = x.astype(BF16)
    return hi, (x - hi.astype(F32)).astype(BF16)


def packed_rows(slots):
    return HALF if slots == SLOTS else TILE


def dot_nn(a, b):
    return lax.dot_general(a, b, (((1,), (0,)), ((), ())), preferred_element_type=F32)


def dot_nt(a, b):
    return lax.dot_general(a, b, (((1,), (1,)), ((), ())), preferred_element_type=F32)


def cols_before(n, s):
    return (n // TILE) * STRIPS + jnp.clip(n % TILE - STRIPS * s, 0, STRIPS)


def column_facts(virt, s, shape):
    w = iota(shape, 1)
    d = w + 77 * div11(w) + STRIPS * s
    block = d >> 6
    before = [cols_before(BLOCK_WIDTH * b, s) for b in range(BLOCKS + 1)]
    labels = [virt[b] for b in range(BLOCKS)]
    label = jnp.zeros(shape, I32)
    rank = w
    for b in range(BLOCKS):
        base = -before[b]
        for e in range(b):
            base = base + jnp.where(labels[e] == labels[b], before[e + 1] - before[e], 0)
        here = block == b
        label = jnp.where(here, labels[b], label)
        rank = jnp.where(here, w + base, rank)
    return d, block, label, rank


def row_label(virt, block, first):
    label = virt[first]
    for k in (1, 2):
        label = jnp.where(block == first + k, virt[jnp.minimum(first + k, BLOCKS - 1)], label)
    return label


def pack_tiles(slots, virt, pair, aux, pat, a_ref, b_ref, d_ref, packed, send_a, send_b):
    r, s, o = coords()
    first = (STRIPS * r) >> 3
    d, block, label, rank = column_facts(virt, s, (1, WIDE))
    sel = jnp.where((iota((128, WIDE), 0) & (slots - 1)) == rank, 1.0, 0.0).astype(BF16)
    left = iota((HALF, 128), 1) < SLOTS

    def pack(src, count, keep, base):
        n = count * STRIPS
        lines = [src[pl.ds(k, n, stride=STRIPS), :] for k in range(STRIPS)]
        for v in range(8):
            start = WIDE * v
            low, off = start // 128, start % 128
            last = (start + WIDE - 1) // 128
            tile = jnp.concatenate(lines[low : last + 1], axis=1)[:, off : off + WIDE]
            hi, lo = split(jnp.where(keep, tile, 0.0))
            d_ref[pl.ds(v, n, stride=8), :] = dot_nt(hi, sel) + dot_nt(lo, sel)
        d_ref[n * 8 : n * 8 + 8, :] = jnp.zeros((8, 128), F32)
        for k in range(count):
            if slots == SLOTS:
                top = d_ref[pl.ds(TILE * k, HALF), :]
                bottom = d_ref[pl.ds(TILE * k + HALF, HALF), :]
                packed[base + k] = jnp.where(left, top, bottom)
            else:
                packed[base + k] = d_ref[pl.ds(TILE * k, TILE), :]

    row = iota((2 * STRIPS, 1), 0)
    p = jnp.where(row >= STRIPS, 1, 0)
    row_block = (STRIPS * r + row - STRIPS * p) >> 3
    keep = label == (row_label(virt, row_block, first) ^ jnp.where(p == 1, pair[1], pair[0]))
    pack(a_ref, 2, keep, 8)
    send_a()

    screens = []
    for k in range(3):
        x = jnp.minimum(first + k, BLOCKS - 1)
        flag = jnp.zeros((1, WIDE), I32)
        for b in range(BLOCKS):
            flag = jnp.where(block == b, pat[x, b] * pat[b, x], flag)
        screens.append(flag)
    row = iota((TILE, 1), 0)
    q = div11(row)
    row_block = (STRIPS * r + row - STRIPS * q) >> 3
    aux_row = jnp.zeros((TILE, 1), I32)
    for k in range(8):
        aux_row = jnp.where(q == k, aux[8 * o + k], aux_row)
    screen = jnp.where(
        row_block == first, screens[0], jnp.where(row_block == first + 1, screens[1], screens[2])
    )
    target = row_label(virt, row_block, first) ^ aux_row
    pack(b_ref, 8, jnp.logical_and(label == target, screen > 0), 0)
    send_b()


def gather_kernel(
    slots, virt, pair, aux, pat, a_ref, b_ref, aa_ref, sa_ref, d_ref, packed, send, recv, near
):
    r, s, o = coords()
    c, x, y = r % 2, (r // 2) % 4, r // 8

    def at(cc, xx, yy, ss):
        return (yy * 8 + xx * 2 + cc, ss, o)

    zs = {k: at(c, x, y, (s + k) % 8) for k in range(1, 8)}
    planes = {
        (e, k): at(c, (x + k) % 4, (y + e) % 2, s) for e in range(2) for k in range(4) if e + k
    }
    sibling = at(1 - c, x, y, s)
    barrier = pltpu.get_barrier_semaphore()
    for peer in [*zs.values(), *planes.values(), sibling]:
        pl.semaphore_signal(barrier, inc=1, device_id=peer, device_id_type=MESH)

    kinds = {}
    copies = []

    def number(kind):
        return kinds.setdefault(kind, len(kinds))

    def describe(src, dst, peer, kind):
        n = number(kind)
        return pltpu.make_async_remote_copy(
            src_ref=src,
            dst_ref=dst,
            send_sem=send.at[n],
            recv_sem=recv.at[n],
            device_id=peer,
            device_id_type=MESH,
        )

    def put(src, dst, peer, *kind):
        copies.append(describe(src, dst, peer, kind))
        copies[-1].start()

    def arrived(ref, *kind):
        describe(ref, ref, sibling, kind).wait_recv()

    def share(ref, *kind):
        put(ref, ref, sibling, "core", *kind)

    def sign(way, k):
        return k if way else -k

    def a_block(k, ch, cc=c):
        return aa_ref.at[cc, 2 * ch : 2 * ch + 2, :, (s + k + 8) % 8]

    def s_block(k, e, cc=c):
        return sa_ref.at[cc, (x + k + 4) % 4, (y + e) % 2]

    def send_a():
        pl.semaphore_wait(barrier, 15)
        for (e, k), peer in planes.items():
            put(packed.at[8 + (y + e) % 2], aa_ref.at[c, x, y, s], peer, "ax", e, k)
        own = pltpu.make_async_copy(packed.at[8 + y], aa_ref.at[c, x, y, s], near.at[0])
        own.start()
        own.wait()

    def send_b():
        for k in (4, 3, 5, 2, 6, 1, 7):
            put(packed.at[(s + k) % 8], sa_ref.at[c, x, y, s], zs[k], "sz", k)
        own = pltpu.make_async_copy(packed.at[s], sa_ref.at[c, x, y, s], near.at[1])
        own.start()
        own.wait()

    pack_tiles(slots, virt, pair, aux, pat, a_ref, b_ref, d_ref, packed, send_a, send_b)

    def a_ring(h):
        for ch in range(2):
            for way in range(2):
                if h:
                    block = a_block(sign(1 - way, h), ch)
                    if h < 4 or ch != way:
                        arrived(block, "az", way, h - 1, ch)
                        share(block, "az", way, h - 1, ch)
                else:
                    block = a_block(0, ch)
                    if way == 0:
                        share(block, "own", ch)
                if h < 3 or (h == 3 and ch != way):
                    put(block, block, zs[1 if way else 7], "az", way, h, ch)

    def s_arrival(e):
        for way in range(2):
            block = s_block(sign(1 - way, 1), e)
            arrived(block, "sx", way, e)
            if e != way:
                put(block, block, planes[0, 1 if way else 3], "sxx", way)
            share(block, "sx", way, e)

    for e, k in planes:
        arrived(aa_ref.at[c, (x - k + 4) % 4, (y + e) % 2, s], "ax", e, k)
    a_ring(0)
    for k in (1, 7, 2, 6, 3, 5, 4):
        arrived(sa_ref.at[c, x, y, (s - k + 8) % 8], "sz", k)
    put(s_block(0, 0), s_block(0, 0), planes[1, 0], "sy")
    for way in range(2):
        put(s_block(0, 0), s_block(0, 0), planes[0, 1 if way else 3], "sx", way, 0)
    share(s_block(0, 0), "sy", 0)
    a_ring(1)
    arrived(s_block(0, 1), "sy")
    for way in range(2):
        put(s_block(0, 1), s_block(0, 1), planes[0, 1 if way else 3], "sx", way, 1)
    share(s_block(0, 1), "sy", 1)
    s_arrival(0)
    a_ring(2)
    s_arrival(1)
    a_ring(3)
    for way in range(2):
        block = s_block(2, 1 - way)
        arrived(block, "sxx", way)
        share(block, "sxx", way)
    a_ring(4)
    for ch in range(2):
        arrived(a_block(0, ch, 1 - c), "core", "own", ch)
        for way in range(2):
            for h in range(4):
                if h < 3 or ch != way:
                    arrived(a_block(sign(1 - way, h + 1), ch, 1 - c), "core", "az", way, h, ch)
    for e in range(2):
        arrived(s_block(0, e, 1 - c), "core", "sy", e)
        for way in range(2):
            arrived(s_block(sign(1 - way, 1), e, 1 - c), "core", "sx", way, e)
    for way in range(2):
        arrived(s_block(2, 1 - way, 1 - c), "core", "sxx", way)
    for copy in copies:
        copy.wait_send()


def product_kernel(
    slots, virt, pair, aux, aa_ref, sa_ref, z_ref, a2, s2, v1, v2, zs, whi, wlo, lists, counts
):
    r, s, o = coords()
    nat, per_label = 8 * slots, slots // 8
    core, x_me, pair_me = r % 2, (r // 2) % 4, r // 8
    h = aux[8 * o + s]
    hp = h ^ pair[pair_me]
    left = iota((HALF, 128), 1) < SLOTS

    def unpack(k, _):
        c, x, y = k % 2, (k // 2) % 4, k // 8
        base = pl.multiple_of(k * TILE, 8)
        for src, dst in ((sa_ref, s2), (aa_ref, a2)):
            if slots != SLOTS:
                for j in range(8):
                    dst[pl.ds(base, TILE), pl.ds(128 * j, 128)] = src[c, x, y, j]
                continue
            for j in range(4):
                even, odd = src[c, x, y, 2 * j], src[c, x, y, 2 * j + 1]
                top = jnp.where(left, even, pltpu.roll(odd, SLOTS, 1))
                bottom = jnp.where(left, pltpu.roll(even, SLOTS, 1), odd)
                dst[pl.ds(base, HALF), pl.ds(128 * j, 128)] = top
                dst[pl.ds(base + HALF, TILE - HALF), pl.ds(128 * j, 128)] = bottom[: TILE - HALF]
        return 0

    lax.fori_loop(0, ROWS, unpack, 0)
    for ref in (s2, a2):
        ref[VIRTUALS:, :] = jnp.zeros((BLOCK_WIDTH, nat), F32)

    for g in range(LABELS):
        counts[g] = 0
        for j in range(per_label):
            lists[per_label * g + j] = BLOCKS
    places = []
    for b in range(BLOCKS):
        g = virt[b]
        n = counts[g]
        lists[per_label * g + jnp.minimum(n, per_label - 1)] = b
        counts[g] = n + 1
        places.append(n)

    group = iota((8, 1), 0)
    d, block, label, rank = column_facts(virt, group, (8, WIDE))
    place = jnp.zeros((8, WIDE), I32)
    for b in range(BLOCKS):
        place = jnp.where(block == b, places[b], place)
    natural = place * BLOCK_WIDTH + (d & (BLOCK_WIDTH - 1))

    tiles = (2 * x_me + core, 8 + 2 * x_me + core)
    bases = [pl.multiple_of(t * TILE, 8) for t in tiles]
    firsts = [(STRIPS * t) >> 3 for t in tiles]
    row = iota((TILE, 1), 0)
    row_blocks = [(t * TILE + row) >> 6 for t in tiles]
    labels = jnp.concatenate([row_label(virt, b, f) for b, f in zip(row_blocks, firsts)], axis=0)

    def to_natural(x, target):
        hi, lo = split(x)
        both = jnp.concatenate([hi, lo], axis=0)
        target = jnp.concatenate([target, target], axis=0)
        total = jnp.zeros((2 * WIDE, nat), F32)
        for k in range(8):
            j, shift = (slots * k) // 128, (slots * k) % 128
            spread = jnp.where(iota((128, WIDE), 0) == rank[k : k + 1] + shift, 1.0, 0.0)
            spread = spread.astype(BF16)
            dense = dot_nn(both[:, 128 * j : 128 * j + 128], spread)
            dense = jnp.where(label[k : k + 1] == target, dense, 0.0).astype(BF16)
            pick = jnp.where(iota((nat, WIDE), 0) == natural[k : k + 1], 1.0, 0.0).astype(BF16)
            total = total + dot_nt(dense, pick)
        return total[:WIDE] + total[WIDE:]

    own = [s2[pl.ds(b, TILE), :] for b in bases]
    own_natural = to_natural(jnp.concatenate(own, axis=0), labels ^ h)

    def load_rows(src, g, half):
        for j in range(4):
            b = lists[per_label * g + 4 * half + j]
            hi, lo = split(src[pl.ds(pl.multiple_of(b * BLOCK_WIDTH, BLOCK_WIDTH), BLOCK_WIDTH), :])
            whi[pl.ds(BLOCK_WIDTH * j, BLOCK_WIDTH), :] = hi
            wlo[pl.ds(BLOCK_WIDTH * j, BLOCK_WIDTH), :] = lo

    def dot3(dot, a):
        hi, lo = split(a)
        return dot(hi, whi[...]) + dot(lo, whi[...]) + dot(hi, wlo[...])

    v1[...] = jnp.zeros_like(v1)
    v2[...] = jnp.zeros_like(v2)
    zs[...] = jnp.zeros_like(zs)
    for t in range(2):
        last = (STRIPS * tiles[t] + STRIPS - 1) >> 3

        def first_product(x, _, t=t):
            g1 = virt[x] ^ h
            g2 = virt[x] ^ hp
            here = row_blocks[t] == x
            mine = jnp.where(here, own[t], 0.0)
            mine_natural = jnp.where(here, own_natural[TILE * t : TILE * t + TILE], 0.0)
            for half in range(nat // 256):
                part = slice(256 * half, 256 * half + 256)

                @pl.when(counts[g1] > 4 * half)
                def _():
                    load_rows(a2, g1, half)
                    v2[t] += dot3(dot_nn, mine_natural[:, part])

                @pl.when(counts[g2] > 4 * half)
                def _():
                    load_rows(a2, g2, half)
                    v1[t, :, part] += dot3(dot_nt, mine)

            return 0

        lax.fori_loop(firsts[t], last + 1, first_product, 0)

    turned = to_natural(jnp.concatenate([v2[0], v2[1]], axis=0), labels ^ hp)
    for t in range(2):
        last = (STRIPS * tiles[t] + STRIPS - 1) >> 3
        y = turned[TILE * t : TILE * t + TILE] - v1[t]

        def second_product(x, _, t=t, y=y):
            g2 = virt[x] ^ hp
            mine = jnp.where(row_blocks[t] == x, y, 0.0)
            for half in range(nat // 256):

                @pl.when(counts[g2] > 4 * half)
                def _():
                    load_rows(s2, g2, half)
                    zs[t, :TILE] += dot3(dot_nn, mine[:, 256 * half : 256 * half + 256])

            return 0

        lax.fori_loop(firsts[t], last + 1, second_product, 0)

    for t in range(2):
        for k in range(8):
            if slots != SLOTS:
                z_ref[t, k] = zs[t, :TILE, pl.ds(128 * k, 128)]
                continue
            j = k // 2
            top = zs[t, 0:HALF, pl.ds(128 * j, 128)]
            bottom = zs[t, HALF : 2 * HALF, pl.ds(128 * j, 128)]
            if k % 2 == 0:
                z_ref[t, k] = jnp.where(left, top, pltpu.roll(bottom, SLOTS, 1))
            else:
                z_ref[t, k] = jnp.where(left, pltpu.roll(top, SLOTS, 1), bottom)


def scatter_kernel(slots, virt, pair, z_ref, out_ref, parts, low_ref, high_ref, send, recv, near):
    r, s, o = coords()
    y, rest = r // 8, r % 8
    alone = jnp.where(y == o, 1, 0)
    barrier = pltpu.get_barrier_semaphore()

    def greet(e, k):
        pl.semaphore_signal(
            barrier, inc=1, device_id=(o * 8 + rest, (s + k) % 8, e), device_id_type=MESH
        )

    def describe(e, k):
        return pltpu.make_async_remote_copy(
            src_ref=z_ref.at[e, (s + k) % 8],
            dst_ref=parts.at[o, s],
            send_sem=send.at[8 * e + k],
            recv_sem=recv.at[8 * o + k],
            device_id=(e * 8 + rest, (s + k) % 8, y),
            device_id_type=MESH,
        )

    def sender(e, k):
        describe(e, k).start()

    def receive(e, k):
        spot = parts.at[e, (s - k + 8) % 8]
        pltpu.make_async_remote_copy(
            src_ref=spot,
            dst_ref=spot,
            send_sem=send.at[0],
            recv_sem=recv.at[8 * e + k],
            device_id=(o * 8 + rest, (s + 1) % 8, e),
            device_id_type=MESH,
        ).wait_recv()

    def finish(e, k):
        describe(e, k).wait_send()

    def each(fn, mine):
        for k in (4, 3, 5, 2, 6, 1, 7, 0):
            for e in range(2):
                if k:
                    fn(e, k)
                else:
                    pl.when(jnp.logical_or(y != o, mine != e))(functools.partial(fn, e, k))

    each(greet, o)
    pl.semaphore_wait(barrier, 16 - alone)
    each(sender, y)

    @pl.when(y == o)
    def _():
        copy = pltpu.make_async_copy(z_ref.at[y, s], parts.at[o, s], near.at[0])
        copy.start()
        copy.wait()

    first = (STRIPS * r) >> 3
    d, block, label, rank = column_facts(virt, s, (1, WIDE))
    each(receive, o)
    total = parts[0, 0]
    for k in range(1, 16):
        total = total + parts[k // 8, k % 8]
    hi, lo = split(0.5 * total)
    rows = packed_rows(slots)
    row = iota((rows, 1), 0)
    for half in range(128 // slots):
        spread = jnp.where(iota((128, WIDE), 0) == rank + slots * half, 1.0, 0.0).astype(BF16)
        dense = dot_nn(hi, spread) + dot_nn(lo, spread)
        row_block = (TILE * r + rows * half + row) >> 6
        keep = label == (row_label(virt, row_block, first) ^ pair[o])
        dense = jnp.where(keep, dense, 0.0)
        low_ref[rows * half : rows * half + rows, :] = dense[:, :128]
        high_ref[rows * half : rows * half + rows, :] = jnp.concatenate(
            [dense[:, 128:], jnp.zeros((rows, 256 - WIDE), F32)], axis=1
        )
    lines = []
    for v in range(8):
        low, high = low_ref[pl.ds(v, STRIPS, stride=8), :], high_ref[pl.ds(v, STRIPS, stride=8), :]
        lines.append(jnp.concatenate([low, high[:, : WIDE - 128]], axis=1))
    for k in range(STRIPS):
        v, w = (128 * k) // WIDE, (128 * k) % WIDE
        piece = lines[v][:, w : min(WIDE, w + 128)]
        if w + 128 > WIDE:
            piece = jnp.concatenate([piece, lines[v + 1][:, : w + 128 - WIDE]], axis=1)
        out_ref[pl.ds(k, STRIPS, stride=STRIPS), :] = piece
    each(finish, y)


def smem(n):
    return [pl.BlockSpec(memory_space=pltpu.SMEM)] * n


def vmem(n):
    return [pl.BlockSpec(memory_space=pltpu.VMEM)] * n


def shape(*dims):
    return jax.ShapeDtypeStruct(dims, F32)


def run_gather(slots, virt, pair, aux, pat, a, b):
    rows = packed_rows(slots)
    full = shape(2, 4, 2, 8, rows, 128)
    return pl.pallas_call(
        functools.partial(gather_kernel, slots),
        out_shape=(full, full),
        in_specs=smem(4) + vmem(2),
        out_specs=tuple(vmem(2)),
        scratch_shapes=[
            pltpu.VMEM((8 * TILE + 8, 128), F32),
            pltpu.VMEM((10, rows, 128), F32),
            pltpu.SemaphoreType.DMA((64,)),
            pltpu.SemaphoreType.DMA((64,)),
            pltpu.SemaphoreType.DMA((2,)),
        ],
        compiler_params=pltpu.CompilerParams(
            collective_id=0 if slots == SLOTS else 2, has_side_effects=True, vmem_limit_bytes=32 * MIB
        ),
    )(virt, pair, aux, pat, a, b)


def run_product(slots, virt, pair, aux, aa, sa):
    nat = 8 * slots
    tall = pltpu.VMEM((VIRTUALS + BLOCK_WIDTH, nat), F32)
    return pl.pallas_call(
        functools.partial(product_kernel, slots),
        out_shape=shape(2, 8, packed_rows(slots), 128),
        in_specs=smem(3) + vmem(2),
        out_specs=vmem(1)[0],
        scratch_shapes=[
            tall,
            tall,
            pltpu.VMEM((2, TILE, nat), F32),
            pltpu.VMEM((2, TILE, nat), F32),
            pltpu.VMEM((2, 2 * HALF, nat), F32),
            pltpu.VMEM((256, nat), BF16),
            pltpu.VMEM((256, nat), BF16),
            pltpu.SMEM((slots,), I32),
            pltpu.SMEM((8,), I32),
        ],
        compiler_params=pltpu.CompilerParams(vmem_limit_bytes=48 * MIB),
    )(virt, pair, aux, aa, sa)


def run_scatter(slots, virt, pair, z):
    return pl.pallas_call(
        functools.partial(scatter_kernel, slots),
        out_shape=shape(121, 128),
        in_specs=smem(2) + vmem(1),
        out_specs=vmem(1)[0],
        scratch_shapes=[
            pltpu.VMEM((2, 8, packed_rows(slots), 128), F32),
            pltpu.VMEM((2 * HALF, 128), F32),
            pltpu.VMEM((2 * HALF, 128), F32),
            pltpu.SemaphoreType.DMA((16,)),
            pltpu.SemaphoreType.DMA((16,)),
            pltpu.SemaphoreType.DMA((1,)),
        ],
        compiler_params=pltpu.CompilerParams(
            collective_id=1 if slots == SLOTS else 3, has_side_effects=True, vmem_limit_bytes=32 * MIB
        ),
    )(virt, pair, z)


def packed_path(slots, amplitudes, aux_factor, virt, pair, aux, pat):
    aa, sa = run_gather(
        slots, virt, pair, aux, pat, amplitudes.reshape(242, 128), aux_factor.reshape(968, 128)
    )
    z = run_product(slots, virt, pair, aux, aa, sa)
    return run_scatter(slots, virt, pair, z).reshape(1, 1, 1, TILE * WIDE)


def widest_label(virt):
    edges = np.arange(BLOCKS + 1)[:, None] * BLOCK_WIDTH
    before = edges // TILE * STRIPS + np.clip(edges % TILE - STRIPS * np.arange(COLS), 0, STRIPS)
    share = jnp.asarray(before[1:] - before[:-1], I32)
    same = virt[:, None] == jnp.arange(LABELS, dtype=I32)
    totals = jnp.sum(jnp.where(same[:, :, None], share[:, None, :], 0), axis=0)
    return jnp.max(totals)


def block_onehot(indices, block_count):
    return indices[..., None] // BLOCK_WIDTH == jnp.arange(block_count, dtype=jnp.int32)


def label_lookup(hot_table, virt_irrep):
    return jnp.sum(jnp.where(hot_table, virt_irrep, 0), axis=-1)


def dense_path(amplitudes, aux_factor, virt_irrep, pair_irrep, aux_irrep, block_pattern):
    tile_count = lax.axis_size("row")
    col_count = lax.axis_size("col")
    local_rows = VIRTUALS // tile_count
    sub_width = local_rows // col_count
    amplitudes = amplitudes.reshape(amplitudes.shape[0], local_rows, tile_count, sub_width)
    aux_factor = aux_factor.reshape(aux_factor.shape[0], local_rows, tile_count, sub_width)
    block_count = virt_irrep.shape[0]
    row_index = lax.axis_index("row") * local_rows + jnp.arange(local_rows, dtype=jnp.int32)
    col_index = (
        jnp.arange(tile_count, dtype=jnp.int32)[:, None] * local_rows
        + lax.axis_index("col") * sub_width
        + jnp.arange(sub_width, dtype=jnp.int32)[None, :]
    )
    row_hot = block_onehot(row_index, block_count)
    col_hot = block_onehot(col_index, block_count)
    product = jnp.bitwise_xor(
        label_lookup(row_hot, virt_irrep)[:, None, None], label_lookup(col_hot, virt_irrep)[None]
    )
    kept_mask = product[None] == pair_irrep[:, None, None, None]
    masked = jnp.where(kept_mask, amplitudes, 0.0)
    pattern = (block_pattern * block_pattern.T).astype(jnp.float32)
    screen = (
        jnp.einsum(
            "ak,kl,itl->ait", row_hot.astype(jnp.float32), pattern, col_hot.astype(jnp.float32)
        )
        > 0.5
    )
    aux_here = aux_factor.shape[0]
    aux_labels = lax.dynamic_slice_in_dim(aux_irrep, lax.axis_index("occ") * aux_here, aux_here, 0)
    aux_mask = jnp.logical_and(screen[None], product[None] == aux_labels[:, None, None, None])
    factor = jnp.where(aux_mask, aux_factor, 0.0)
    half_pairs = masked.shape[0] // lax.axis_size("occ")
    masked = lax.dynamic_slice_in_dim(masked, lax.axis_index("occ") * half_pairs, half_pairs, 0)
    factor = lax.all_gather(factor, "occ", axis=0, tiled=True)
    pair_count = masked.shape[0]
    aux_count = factor.shape[0]
    split_view = masked.reshape(pair_count, col_count, sub_width, tile_count, sub_width)
    swapped = lax.all_to_all(
        lax.all_to_all(split_view, "row", split_axis=3, concat_axis=3, tiled=True),
        "col",
        split_axis=1,
        concat_axis=4,
        tiled=True,
    )
    mirrored = swapped.reshape(pair_count, sub_width, tile_count, local_rows).transpose(0, 3, 2, 1)
    antisym = masked - mirrored
    columns = lax.all_gather(factor, "row", axis=1, tiled=True)
    columns = columns.reshape(aux_count, tile_count, local_rows, tile_count * sub_width)
    rows_panel = lax.all_gather(factor, "col", axis=3, tiled=True).reshape(
        aux_count, local_rows, tile_count * local_rows
    )
    chosen = columns
    contracted = jnp.einsum(
        "pcik,qikn->qpcn",
        lax.all_gather(antisym, "col", axis=3, tiled=True),
        chosen,
        precision=lax.Precision.HIGHEST,
    )
    chosen = rows_panel
    summed = lax.psum_scatter(
        jnp.einsum("qca,qpcn->apn", chosen, contracted, precision=lax.Precision.HIGHEST),
        "row",
        scatter_dimension=0,
        tiled=True,
    )
    pairs_out = summed.shape[1]
    result = (
        (0.5 * summed).reshape(local_rows, pairs_out, tile_count, sub_width).transpose(1, 0, 2, 3)
    )
    return result.reshape(pairs_out, 1, 1, local_rows * tile_count * sub_width)


def per_device(*args):
    widest = widest_label(args[2])
    paths = [functools.partial(packed_path, SLOTS), functools.partial(packed_path, 128), dense_path]
    which = jnp.where(widest > SLOTS, 1, 0) + jnp.where(widest > 128, 1, 0)
    return lax.switch(which, paths, *args)


def solution(mesh):
    placed = (P(None, "row", "col", None), P("occ", "row", "col", None), P(), P(), P(), P())
    return jax.shard_map(
        per_device,
        mesh=mesh,
        in_specs=placed,
        out_specs=P("occ", "row", "col", None),
        check_vma=False,
    )
```

time: 113 us -> 88.7 us (0.78); the launches traced: 113 us -> 86.9 us
  Pallas kernels: 89.6 us -> 66 us
  local copies, waits for them, and re-layouts: 5.67 us -> 2.45 us
    pallas_call x5 -> x3, Pallas kernels: 89.6 us -> 66 us  [the longest x1 35.3 us: run_gather(): pl.pallas_call(functools.partial(gather_kernel, slots), out_shape=(full,...]
    cond x14 -> x6, local copies, waits for them, and re-layouts: 4.89 us -> 1.67 us
where the time goes in v2:
time: 88.7 us; the launch traced here: 86.9 us
  Pallas kernels  66 us (74%)
  between operations  14.7 us (17%)
  other arithmetic  3.46 us (4%)
  local copies, waits for them, and re-layouts  2.45 us (3%)
    pallas_call x1, Pallas kernels, run_gather(): pl.pallas_call(functools.partial(gather_kernel, slots), out_shape=(full,...  35.3 us
    pallas_call x1, Pallas kernels, run_product(): pl.pallas_call(functools.partial(product_kernel, slots), out_shape=shape(...  15.5 us
    pallas_call x1, Pallas kernels, run_scatter(): pl.pallas_call(functools.partial(scatter_kernel, slots), out_shape=shape(...  15.2 us

profile of v2, /device:TPU:5, one launch (start us, length us, event | category | flops | bytes accessed | tf_op | source)
XLA Modules:
  0.0 86.9 jit_solution(2261973943516241636)
XLA Ops:
  6.5 0.7 iota_compare_fusion.5
  7.2 0.9 %select_reduce_fusion.2 = s32[8,8]{1,0:T(8,128)S(1)} fusion(s32[22,8]{0,1:T(8,128)} %constant.69.clone, pred[22,8]{0,1:T(8,128)(4,1)S(1)} %iota_compare_fusion.5), kind=kLoop, calls=%fused_computation.33 | loop fusion | flops 2752 | bytes 1136 | tf_op jit(solution)/shard_map/reduce_sum | solution.py:595
  8.1 0.6 reduce_max.9
  10.0 69.4 %conditional.1 = (f32[1,1,1,15488]{3,2,1,0:T(1,128)S(1)}) conditional(s32[]{:T(128)} %clamp.3, (f32[2,1,1,15488]{3,2,1,0:T(1,128)}, f32[8,1,1,15488]{3,2,1,0:T(1,128)}, s32[22]{0:T(128)}, s32[2]{0:T(128)}, s32[16]{0:T(128)}, /*index=5*/s32[22,22]{1,0:T(8,128)}) %tuple.14, (f32[2,1,1,15488]{3,2,1,0:T(1,128)}, ...), branch_computations={%region_2.3_spmd, %region_3.4_spmd, %region_4.8_spmd} | conditional | flops 8375187456 | bytes 371862720 | solution.py:684
  10.1 0.0 copy-start.6
  10.1 0.0 copy-start.8
  10.1 1.3 %reduce = f32[2,15488]{1,0:T(2,128)S(1)} reduce(f32[2,1,1,15488]{3,2,1,0:T(1,128)} %get-tuple-element.140, f32[]{:T(128)} %constant.72), dimensions={1,2}, to_apply=%get-tuple-element.140.reduce_sub_computation | reduce | bytes 247812 | tf_op jit(solution)/shard_map
  11.3 0.1 reshape.158.a_ref
  11.5 35.3 %branch_0_fun.3 = (f32[2,4,2,8,48,128]{5,4,3,2,1,0:T(8,128)S(1)}, f32[2,4,2,8,48,128]{5,4,3,2,1,0:T(8,128)S(1)}) custom-call(s32[22]{0:T(128)} %get-tuple-element.44.virt, s32[2]{0:T(128)} %get-tuple-element.46.pair, s32[16]{0:T(128)} %get-tuple-element.47.aux, s32[22,22]{1,0:T(8,128)} %get-tuple-element.48.pat, f32[242,128]{1,0:T(8,128)S(1)} %reshape.158.a_ref, ...), custom_call_target="tpu_custom_call" | custom-call | tf_op jit(solution)/shard_map/cond/branch_0_fun/pallas_call | solution.py:521
  46.8 0.0 copy-start.2
  46.8 1.7 %copy-done.2 = f32[2,4,2,8,48,128]{5,4,3,2,1,0:T(8,128)} copy-done((f32[2,4,2,8,48,128]{5,4,3,2,1,0:T(8,128)}, f32[2,4,2,8,48,128]{5,4,3,2,1,0:T(8,128)S(1)}, u32[]{:S(2)}) %copy-start.2) | copy-done | bytes 3145752 | tf_op jit(solution)/shard_map/cond
  48.5 15.5 %branch_0_fun.4.z_ref = f32[2,8,48,128]{3,2,1,0:T(8,128)S(1)} custom-call(s32[22]{0:T(128)} %get-tuple-element.44.virt, s32[2]{0:T(128)} %get-tuple-element.46.pair, s32[16]{0:T(128)} %get-tuple-element.47.aux, f32[2,4,2,8,48,128]{5,4,3,2,1,0:T(8,128)S(1)} %get-tuple-element.51.aa_ref, f32[2,4,2,8,48,128]{5,4,3,2,1,0:T(8,128)} %copy-done.2), custom_call_target="tpu_custom_call" | custom-call | tf_op jit(solution)/shard_map/cond/branch_0_fun/pallas_call | solution.py:542
  63.9 0.0 copy-done.6
  63.9 0.0 copy-done.8
  63.9 15.2 %branch_0_fun.5 = f32[121,128]{1,0:T(8,128)S(1)} custom-call(s32[22]{0:T(128)S(1)} %copy-done.6, s32[2]{0:T(128)S(1)} %copy-done.8, f32[2,8,48,128]{3,2,1,0:T(8,128)S(1)} %branch_0_fun.4.z_ref), custom_call_target="tpu_custom_call" | custom-call | tf_op jit(solution)/shard_map/cond/branch_0_fun/pallas_call | solution.py:563
  79.2 0.1 reshape.160
  79.5 0.0 copy-start.5
  79.5 0.6 copy-done.5
Async XLA Ops:
  10.1 53.9 %copy-start.6 = (s32[22]{0:T(128)S(1)}, s32[22]{0:T(128)}, u32[]{:S(2)}) copy-start(s32[22]{0:T(128)} %get-tuple-element.44.virt) | copy-start | bytes 268 | tf_op jit(solution)/shard_map/cond
  10.1 53.9 %copy-start.8 = (s32[2]{0:T(128)S(1)}, s32[2]{0:T(128)}, u32[]{:S(2)}) copy-start(s32[2]{0:T(128)} %get-tuple-element.46.pair) | copy-start | bytes 28 | tf_op jit(solution)/shard_map/cond
  46.8 1.7 %copy-start.2 = (f32[2,4,2,8,48,128]{5,4,3,2,1,0:T(8,128)}, f32[2,4,2,8,48,128]{5,4,3,2,1,0:T(8,128)S(1)}, u32[]{:S(2)}) copy-start(f32[2,4,2,8,48,128]{5,4,3,2,1,0:T(8,128)S(1)} %get-tuple-element.52.sa_ref) | copy-start | bytes 9437188 | tf_op jit(solution)/shard_map/cond
  79.5 0.6 copy-start.5
